TPU v7x, 512 devices: a whole 4x4x16 slice. The times are simulated.
512 devices in a mesh: space: 32 (over z, core), mode: 16 (over y, x).
Axes of the slice: x: 4, y: 4, z: 16, core: 2. Of those that a mesh axis runs over, the one named last changes fastest.
Arguments:
- basis: float32 [3, 256, 16, 8, 2048], P(None, 'space', None, None, 'mode'), may hold values from -132 to 132
- mean_flow: float32 [3, 256, 16, 8], P(None, 'space'), may hold values from -3 to 3
- flow_gradient: float32 [3, 3, 256, 16, 8], P(None, None, 'space'), may hold values from -2 to 2
- viscosity: float32 [256, 16, 8], P('space'), may hold values from 0.02 to 0.2
Outputs:
- reduced: float32 [2048, 2048], P('mode', 'space')
- advected: float32 [3, 256, 16, 8, 2048], P(None, 'space', None, None, 'mode')
- r_factor: float32 [2048, 128], P('mode')
All inputs are finite; a program needn't handle non-finite values.
Results may differ from a plain program's by a relative error of at most 0.00074.
Values may be sent and summed in bfloat16 or wider, within the bound.
No kernel may reach another device: no remote copies, remote signals or barrier semaphores. Data moves between devices by JAX's collectives and lax.ppermute only.
A program may use at most 64 MiB of HBM per device.

v0:
```python
import jax
import jax.numpy as jnp
from jax import lax
from jax.sharding import PartitionSpec as P


def extended(cells, sides, width):
    for axis, dim in sides:
        count = lax.axis_size(axis)
        ends = count - 1
        head = lax.slice_in_dim(cells, 0, width, axis=dim)
        tail = lax.slice_in_dim(cells, cells.shape[dim] - width, cells.shape[dim], axis=dim)
        cells = jnp.concatenate(
            [
                lax.ppermute(tail, axis, [(i, (i + 1) % count) for i in range(ends)]),
                cells,
                lax.ppermute(head, axis, [((i + 1) % count, i) for i in range(ends)]),
            ],
            axis=dim,
        )
    return cells


def transport(padded, mean_flow, flow_gradient, viscosity):
    center = padded[:, 1:-1]
    widen_y = jnp.pad(center, ((0, 0), (0, 0), (1, 1), (0, 0), (0, 0)))
    widen_z = jnp.pad(center, ((0, 0), (0, 0), (0, 0), (1, 1), (0, 0)))
    east_side = padded[:, 2:]
    west_side = padded[:, :-2]
    north_side = widen_y[:, :, 2:]
    south_side = widen_y[:, :, :-2]
    upper_side = widen_z[:, :, :, 2:]
    lower_side = widen_z[:, :, :, :-2]
    laplacian = (
        east_side + west_side + north_side + south_side + upper_side + lower_side - 6.0 * center
    )
    advection = 0.5 * (
        mean_flow[0][None, :, :, :, None] * (east_side - west_side)
        + mean_flow[1][None, :, :, :, None] * (north_side - south_side)
        + mean_flow[2][None, :, :, :, None] * (upper_side - lower_side)
    )
    coupling = flow_gradient[:, 0][..., None] * center[0][None]
    coupling = coupling + flow_gradient[:, 1][..., None] * center[1][None]
    coupling = coupling + flow_gradient[:, 2][..., None] * center[2][None]
    return viscosity[None, :, :, :, None] * laplacian - advection - coupling


def apply_inverse(field, lower_factor):
    width = field.shape[4]
    flat_rows = field.reshape(-1, width)
    solved = jax.scipy.linalg.solve_triangular(lower_factor, flat_rows.T, lower=True)
    return solved.T.reshape(field.shape)


def body(basis, mean_flow, flow_gradient, viscosity):
    cells_x = basis.shape[1]
    cells_y = basis.shape[2]
    cells_z = basis.shape[3]
    panel_width = basis.shape[4]
    weight = 1.0 / (3 * cells_x * cells_y * cells_z * lax.axis_size("space"))
    flat_basis = basis.reshape(-1, panel_width)
    gram_local = (
        jnp.dot(
            flat_basis.T,
            flat_basis,
            precision=lax.Precision.HIGHEST,
            preferred_element_type=jnp.float32,
        )
        * weight
    )
    gram = lax.psum(gram_local, "space")
    lower_factor = jnp.linalg.cholesky(gram)
    ortho = apply_inverse(basis, lower_factor)
    padded_ortho = extended(ortho, (("space", 1),), 1)
    advected = transport(padded_ortho, mean_flow, flow_gradient, viscosity)
    rounded_images = advected.astype(jnp.bfloat16)
    rounded_rows = ortho.astype(jnp.bfloat16).reshape(-1, panel_width)
    panel_piece = lax.all_gather(rounded_images, "mode", axis=4, tiled=True)
    piece_rows = panel_piece.reshape(-1, panel_piece.shape[4])
    strip = (
        jnp.einsum("ra,rk->ak", rounded_rows, piece_rows, preferred_element_type=jnp.float32)
        * weight
    )
    reduced = lax.psum_scatter(strip, "space", scatter_dimension=1, tiled=True)
    return (reduced, advected, lower_factor.T)


def solution(mesh):
    placed = (
        P(None, "space", None, None, "mode"),
        P(None, "space", None, None),
        P(None, None, "space", None, None),
        P("space", None, None),
    )
    return jax.shard_map(
        body,
        mesh=mesh,
        in_specs=placed,
        out_specs=(P("mode", "space"), P(None, "space", None, None, "mode"), P("mode", None)),
        check_vma=False,
    )
```

profile of v0, /device:TPU:2, one launch (start us, length us, event | category | flops | bytes accessed | tf_op | source)
XLA Modules:
  0.0 491.2 jit_solution(15039007794072252386)
XLA Ops:
  7.2 0.0 all-reduce.4.cloned.1.call-start
  7.2 1.3 copy-done
  8.6 3.3 fusion.8
  11.9 0.0 all-gather.2.cloned.1.call-start
  12.0 0.6 slice_bitcast_fusion.5
  12.6 186.8 %all-reduce.4.cloned.1.call-done = f32[128,128]{0,1:T(8,128)} async-done(((f32[128,128]{0,1:T(8,128)}), f32[128,128]{0,1:T(8,128)}) %all-reduce.4.cloned.1.call-update) | async-done | bytes 65552 | tf_op jit(solution)/shard_map/psum | solution.py:71
  199.4 0.9 copy.27
  200.3 0.9 fusion.11
  201.2 11.7 %cholesky.16 = f32[128,128]{1,0:T(8,128)S(1)} custom-call(f32[128,128]{1,0:T(8,128)S(1)} %fusion.11), custom_call_target="Cholesky" | custom-call | tf_op jit(solution)/shard_map/jit(cholesky)/cholesky | solution.py:72
  212.9 0.6 compare_reduce_fusion
  213.5 0.7 fusion.12
  214.2 10.4 %custom-call.7 = f32[1,128,128]{1,2,0:T(8,128)} custom-call(f32[1,128,128]{2,1,0:T(8,128)S(1)} %get-tuple-element.23), custom_call_target="InvertDiagBlocksLowerTriangular" | custom-call | tf_op jit(solution)/shard_map/jit(_solve_triangular)/triangular_solve | solution.py:51
  224.7 2.3 convolution_bitcast_fusion
  227.0 1.6 copy.28
  228.6 1.7 copy.30
  230.3 0.8 fusion.14
  231.1 1.3 collective-permute-start
  232.4 3.7 collective-permute-start.1
  236.1 1.2 fusion.15
  237.3 1.3 copy.36
  238.6 0.9 copy.37
  239.5 1.0 copy.40
  240.5 2.1 copy.41
  242.6 2.1 copy.38
  244.7 1.1 copy.39
  245.8 4.9 %fusion.13 = (bf16[3,8,16,8,128]{4,2,3,1,0:T(8,128)(2,1)}, f32[3,8,16,8,128]{4,2,3,1,0:T(8,128)}) fusion(f32[8,16,8,128]{3,1,2,0:T(8,128)} %copy.41, f32[3,8,16,8]{2,3,1,0:T(8,128)S(1)} %get-tuple-element.17, f32[8,16,8,128]{3,1,2,0:T(8,128)S(1)} %copy.39, f32[3,8,16,8]{2,3,1,0:T(8,128)S(1)} %get-tuple-element.18, f32[8,16,8,128]{3,1,2,0:T(8,128)} %copy.37, ...), kind=kLoop, calls=%fused_computation.31 | loop fusion | flops 10616832 | bytes 5951488 | tf_op jit(solution)/shard_map/convert_element_type | solution.py:76
  250.8 0.0 reduce-scatter.2.cloned.1.call-start
  250.9 110.3 %all-gather.2.cloned.1.call-done = bf16[3,8,16,8,2048]{4,2,3,1,0:T(8,128)(2,1)} async-done(((bf16[3,8,16,8,128]{4,2,3,1,0:T(8,128)(2,1)}), bf16[3,8,16,8,2048]{4,2,3,1,0:T(8,128)(2,1)}) %all-gather.2.cloned.1.call-update) | async-done | bytes 12582928 | tf_op jit(solution)/shard_map/all_gather | solution.py:78
  361.1 15.4 %fusion.5 = f32[128,2048]{0,1:T(8,128)} fusion(bf16[3,8,16,8,2048]{4,2,3,1,0:T(8,128)(2,1)} %all-gather.2.cloned.1.call-done, f32[3,8,16,8,128]{4,3,2,1,0:T(8,128)} %bitcast.45), kind=kOutput, calls=%fused_computation.6 | convolution fusion | flops 1611268096 | bytes 15204352 | tf_op jit(solution)/shard_map/ra,rk->ak/dot_general | solution.py:81
  376.6 0.7 copy.44
  377.3 1.7 copy.43
  379.1 105.6 %reduce-scatter.2.cloned.1.call-done = f32[128,64]{0,1:T(8,128)} async-done(((f32[128,2048]{0,1:T(8,128)}), f32[128,64]{0,1:T(8,128)}) %reduce-scatter.2.cloned.1.call-update) | async-done | bytes 32784 | tf_op jit(solution)/shard_map/reduce_scatter | solution.py:84
  (20 shorter events, 0.1 us)
Async XLA Ops:
  7.2 1.4 copy-start
  7.2 4.7 copy-start.5
  7.2 4.8 copy-start.6
  7.2 192.2 %all-reduce.4.cloned.1.call-start = ((), (), s32[]{:S(2)}) async-start(), calls=%async_computation.1 | async-start | bytes 131072 | tf_op jit(solution)/shard_map/psum | solution.py:71
  11.9 349.3 %all-gather.2.cloned.1.call-start = ((), (), s32[]{:S(2)}) async-start(), calls=%async_computation.2 | async-start | bytes 13369344 | tf_op jit(solution)/shard_map/all_gather | solution.py:78
  230.3 7.0 %copy-start.1 = (f32[3,8,16,8,128]{4,2,3,1,0:T(8,128)}, f32[3,8,16,8,128]{4,2,3,1,0:T(8,128)S(1)}, u32[]{:S(2)}) copy-start(f32[3,8,16,8,128]{4,2,3,1,0:T(8,128)S(1)} %copy.30) | copy-start | bytes 4718596
  231.1 14.7 %collective-permute-start = (f32[3,1,16,8,128]{4,2,3,1,0:T(8,128)}, f32[3,1,16,8,128]{4,2,3,1,0:T(8,128)}, u32[]{:S(2)}, u32[]{:S(2)}) collective-permute-start(f32[3,1,16,8,128]{4,2,3,1,0:T(8,128)} %get-tuple-element.11), channel_id=1, source_target_pairs={{16,0},{32,16},{48,32},{64,48},{80,64},{96,80},{112,96},{128,112},... | collective-permute-start | bytes 589832 | tf_op jit(solution)/shard_map/ppermute | solution.py:17
  232.4 13.4 %collective-permute-start.1 = (f32[3,1,16,8,128]{4,2,3,1,0:T(8,128)}, f32[3,1,16,8,128]{4,2,3,1,0:T(8,128)}, u32[]{:S(2)}, u32[]{:S(2)}) collective-permute-start(f32[3,1,16,8,128]{4,2,3,1,0:T(8,128)} %get-tuple-element.12), channel_id=1, source_target_pairs={{0,16},{16,32},{32,48},{48,64},{64,80},{80,96},{96,112},{112,128},... | collective-permute-start | bytes 589832 | tf_op jit(solution)/shard_map/ppermute | solution.py:15
  237.3 2.2 copy-start.4
  240.5 5.3 %copy-start.2 = (f32[3,8,16,8,128]{4,2,3,1,0:T(8,128)S(1)}, f32[3,8,16,8,128]{4,2,3,1,0:T(8,128)}, u32[]{:S(2)}) copy-start(f32[3,8,16,8,128]{4,2,3,1,0:T(8,128)} %copy-done.1) | copy-start | bytes 4718596
  250.8 233.9 %reduce-scatter.2.cloned.1.call-start = ((), (), s32[]{:S(2)}) async-start(), calls=%async_computation.3 | async-start | bytes 1081344 | tf_op jit(solution)/shard_map/reduce_scatter | solution.py:84
  361.1 16.2 %copy-start.3 = (f32[3,8,16,8,128]{4,2,3,1,0:T(8,128)S(1)}, f32[3,8,16,8,128]{4,2,3,1,0:T(8,128)}, u32[]{:S(2)}) copy-start(f32[3,8,16,8,128]{4,2,3,1,0:T(8,128)} %get-tuple-element.10) | copy-start | bytes 4718596
Sparse Core Ops, SparseCore 0:
  12.0 187.3 all-reduce.3
  250.9 110.1 all-gather.1
  376.7 107.9 reduce-scatter.1
where the time goes:
time: 492 us; the launch traced here: 491 us
  waiting for transfers between devices  403 us (82%)
  other arithmetic  29.3 us (6%)
  matrix products  21 us (4%)
  local copies, waits for them, and re-layouts  19.2 us (4%)
  between operations  13.9 us (3%)
  starting transfers between devices  5.11 us (1%)
    psum x1, waiting for transfers between devices, body(): gram = lax.psum(gram_local, 'space')  187 us
    all_gather x1, waiting for transfers between devices, body(): panel_piece = lax.all_gather(rounded_images, 'mode', axis=4, tiled=True)  110 us
    reduce_scatter x1, waiting for transfers between devices, body(): reduced = lax.psum_scatter(strip, 'space', scatter_dimension=1, tiled=True)  106 us
    dot_general x1, matrix products, body(): jnp.einsum('ra,rk->ak', rounded_rows, piece_rows, preferred_element_type=...  15.4 us
    another operation x3, other arithmetic, body(): lower_factor = jnp.linalg.cholesky(gram)  12.4 us
    another operation x1, other arithmetic, apply_inverse(): jax.scipy.linalg.solve_triangular(lower_factor, flat_rows.T, lower=True)  10.4 us
  transfers between devices with their start and end apart: 5, of which 3 were waited for; matrix products, arithmetic and copies ran while one was open for 3% of the time, Pallas kernels for 0%

commit v1 on v0

--- a/solution.py
+++ b/solution.py
@@ -2,6 +2,14 @@
 import jax.numpy as jnp
 from jax import lax
 from jax.sharding import PartitionSpec as P
+
+
+def sum_by_hops(x, axis):
+    size, acc = (lax.axis_size(axis), x)
+    for stride in [1 << k for k in range(size.bit_length() - 1)]:
+        route = [(i, i ^ stride) for i in range(size)]
+        acc = acc + lax.ppermute(acc, axis, route)
+    return acc
 
 
 def extended(cells, sides, width):
@@ -68,7 +76,7 @@
         )
         * weight
     )
-    gram = lax.psum(gram_local, "space")
+    gram = sum_by_hops(gram_local, "space")
     lower_factor = jnp.linalg.cholesky(gram)
     ortho = apply_inverse(basis, lower_factor)
     padded_ortho = extended(ortho, (("space", 1),), 1)

time: 492 us -> 355 us (0.72)
  waiting for transfers between devices: 403 us -> 234 us
  starting transfers between devices: 5.11 us -> 38.9 us
    psum x1 -> x0, waiting for transfers between devices: 187 us -> none  [body(): gram = lax.psum(gram_local, 'space')]
    ppermute x0 -> x5, starting transfers between devices: none -> 33.8 us  [sum_by_hops(): acc = acc + lax.ppermute(acc, axis, route)]
    ppermute x0 -> x5, waiting for transfers between devices: none -> 14 us  [sum_by_hops(): acc = acc + lax.ppermute(acc, axis, route)]
  transfers between devices with their start and end apart: 5 -> 9, of which waited for: 3 -> 7; matrix products, arithmetic and copies ran while one was open for 3% -> 4% of each run, Pallas kernels for 0% -> 0%
where the time goes in v1:
time: 355 us; the launch traced here: 354 us
  waiting for transfers between devices  234 us (66%)
  starting transfers between devices  38.9 us (11%)
  other arithmetic  28.5 us (8%)
  matrix products  20.4 us (6%)
  local copies, waits for them, and re-layouts  18.3 us (5%)
  between operations  14.2 us (4%)
    all_gather x1, waiting for transfers between devices, body(): panel_piece = lax.all_gather(rounded_images, 'mode', axis=4, tiled=True)  114 us
    reduce_scatter x1, waiting for transfers between devices, body(): reduced = lax.psum_scatter(strip, 'space', scatter_dimension=1, tiled=True)  106 us
    ppermute x5, starting transfers between devices, sum_by_hops(): acc = acc + lax.ppermute(acc, axis, route)  33.8 us
    dot_general x1, matrix products, body(): jnp.einsum('ra,rk->ak', rounded_rows, piece_rows, preferred_element_type=...  15.4 us
    ppermute x5, waiting for transfers between devices, sum_by_hops(): acc = acc + lax.ppermute(acc, axis, route)  14 us
    another operation x3, other arithmetic, body(): lower_factor = jnp.linalg.cholesky(gram)  12.4 us
    another operation x1, other arithmetic, apply_inverse(): jax.scipy.linalg.solve_triangular(lower_factor, flat_rows.T, lower=True)  10.4 us
  transfers between devices with their start and end apart: 9, of which 7 were waited for; matrix products, arithmetic and copies ran while one was open for 4% of the time, Pallas kernels for 0%

profile of v1, /device:TPU:2, one launch (start us, length us, event | category | flops | bytes accessed | tf_op | source)
XLA Modules:
  0.0 354.2 jit_solution(15361587352545713712)
XLA Ops:
  7.2 1.3 copy-done
  8.6 2.6 fusion.8
  11.2 1.9 collective-permute-start
  13.1 1.2 collective-permute-done
  14.4 3.8 %collective-permute-start.1 = (f32[128,128]{0,1:T(8,128)S(1)}, f32[128,128]{0,1:T(8,128)S(1)}, u32[]{:S(2)}, u32[]{:S(2)}) collective-permute-start(f32[128,128]{0,1:T(8,128)S(1)} %add.60), channel_id=1, source_target_pairs={{0,32},{16,48},{32,0},{48,16},{64,96},{80,112},{96,64},{112,80},{1... | collective-permute-start | bytes 196616 | tf_op jit(solution)/shard_map/ppermute | solution.py:11
  18.2 2.4 collective-permute-done.1
  20.6 5.2 %collective-permute-start.2 = (f32[128,128]{0,1:T(8,128)S(1)}, f32[128,128]{0,1:T(8,128)S(1)}, u32[]{:S(2)}, u32[]{:S(2)}) collective-permute-start(f32[128,128]{0,1:T(8,128)S(1)} %add.61), channel_id=1, source_target_pairs={{0,64},{16,80},{32,96},{48,112},{64,0},{80,16},{96,32},{112,48},{1... | collective-permute-start | bytes 196616 | tf_op jit(solution)/shard_map/ppermute | solution.py:11
  25.8 2.5 collective-permute-done.2
  28.4 9.1 %collective-permute-start.3 = (f32[128,128]{0,1:T(8,128)S(1)}, f32[128,128]{0,1:T(8,128)S(1)}, u32[]{:S(2)}, u32[]{:S(2)}) collective-permute-start(f32[128,128]{0,1:T(8,128)S(1)} %add.62), channel_id=1, source_target_pairs={{0,128},{16,144},{32,160},{48,176},{64,192},{80,208},{96,224},{112... | collective-permute-start | bytes 196616 | tf_op jit(solution)/shard_map/ppermute | solution.py:11
  37.5 4.8 %collective-permute-done.3 = f32[128,128]{0,1:T(8,128)S(1)} collective-permute-done((f32[128,128]{0,1:T(8,128)S(1)}, f32[128,128]{0,1:T(8,128)S(1)}, u32[]{:S(2)}, u32[]{:S(2)}) %collective-permute-start.3) | collective-permute-done | bytes 65568 | tf_op jit(solution)/shard_map/ppermute | solution.py:11
  42.4 13.8 %collective-permute-start.4 = (f32[128,128]{0,1:T(8,128)S(1)}, f32[128,128]{0,1:T(8,128)S(1)}, u32[]{:S(2)}, u32[]{:S(2)}) collective-permute-start(f32[128,128]{0,1:T(8,128)S(1)} %add.63), channel_id=1, source_target_pairs={{0,256},{16,272},{32,288},{48,304},{64,320},{80,336},{96,352},{112... | collective-permute-start | bytes 196616 | tf_op jit(solution)/shard_map/ppermute | solution.py:11
  56.8 3.0 collective-permute-done.4
  59.9 11.7 %cholesky.16 = f32[128,128]{1,0:T(8,128)S(1)} custom-call(f32[128,128]{1,0:T(8,128)S(1)} %fusion.11), custom_call_target="Cholesky" | custom-call | tf_op jit(solution)/shard_map/jit(cholesky)/cholesky | solution.py:80
  72.9 10.4 %custom-call.7 = f32[1,128,128]{1,2,0:T(8,128)} custom-call(f32[1,128,128]{2,1,0:T(8,128)S(1)} %get-tuple-element.23), custom_call_target="InvertDiagBlocksLowerTriangular" | custom-call | tf_op jit(solution)/shard_map/jit(_solve_triangular)/triangular_solve | solution.py:59
  83.4 2.3 convolution_bitcast_fusion
  85.7 1.6 copy.28
  87.3 1.7 copy.30
  89.0 0.8 fusion.14
  89.9 1.3 collective-permute-start.5
  91.2 3.7 %collective-permute-start.6 = (f32[3,1,16,8,128]{4,2,3,1,0:T(8,128)}, f32[3,1,16,8,128]{4,2,3,1,0:T(8,128)}, u32[]{:S(2)}, u32[]{:S(2)}) collective-permute-start(f32[3,1,16,8,128]{4,2,3,1,0:T(8,128)} %get-tuple-element.12), channel_id=1, source_target_pairs={{0,16},{16,32},{32,48},{48,64},{64,80},{80,96},{96,112},{112,128},... | collective-permute-start | bytes 589832 | tf_op jit(solution)/shard_map/ppermute | solution.py:23
  94.9 1.2 fusion.15
  96.1 1.3 copy.36
  97.4 0.9 copy.37
  98.3 1.0 copy.40
  99.3 2.1 copy.41
  101.4 2.0 copy.38
  103.4 1.1 copy.39
  104.6 4.9 %fusion.13 = (bf16[3,8,16,8,128]{4,2,3,1,0:T(8,128)(2,1)}, f32[3,8,16,8,128]{4,2,3,1,0:T(8,128)}) fusion(f32[8,16,8,128]{3,1,2,0:T(8,128)} %copy.41, f32[3,8,16,8]{2,3,1,0:T(8,128)S(1)} %get-tuple-element.17, f32[8,16,8,128]{3,1,2,0:T(8,128)S(1)} %copy.39, f32[3,8,16,8]{2,3,1,0:T(8,128)S(1)} %get-tuple-element.18, f32[8,16,8,128]{3,1,2,0:T(8,128)} %copy.37, ...), kind=kLoop, calls=%fused_computation.31 | loop fusion | flops 10616832 | bytes 5951488 | tf_op jit(solution)/shard_map/convert_element_type | solution.py:84
  109.6 114.2 %all-gather.2.cloned.1.call-done = bf16[3,8,16,8,2048]{4,2,3,1,0:T(8,128)(2,1)} async-done(((bf16[3,8,16,8,128]{4,2,3,1,0:T(8,128)(2,1)}), bf16[3,8,16,8,2048]{4,2,3,1,0:T(8,128)(2,1)}) %all-gather.2.cloned.1.call-update) | async-done | bytes 12582928 | tf_op jit(solution)/shard_map/all_gather | solution.py:86
  223.8 15.4 %fusion.5 = f32[128,2048]{0,1:T(8,128)} fusion(bf16[3,8,16,8,2048]{4,2,3,1,0:T(8,128)(2,1)} %all-gather.2.cloned.1.call-done, f32[3,8,16,8,128]{4,3,2,1,0:T(8,128)} %bitcast.45), kind=kOutput, calls=%fused_computation.6 | convolution fusion | flops 1611268096 | bytes 15204352 | tf_op jit(solution)/shard_map/ra,rk->ak/dot_general | solution.py:89
  240.0 1.7 copy.43
  241.7 105.6 %reduce-scatter.2.cloned.1.call-done = f32[128,64]{0,1:T(8,128)} async-done(((f32[128,2048]{0,1:T(8,128)}), f32[128,64]{0,1:T(8,128)}) %reduce-scatter.2.cloned.1.call-update) | async-done | bytes 32784 | tf_op jit(solution)/shard_map/reduce_scatter | solution.py:92
  (32 shorter events, 3.0 us)
Async XLA Ops:
  7.2 1.4 copy-start
  7.2 30.3 %copy-start.5 = (f32[3,3,8,16,8]{3,4,2,1,0:T(8,128)S(1)}, f32[3,3,8,16,8]{3,4,2,1,0:T(8,128)}, u32[]{:S(2)}) copy-start(f32[3,3,8,16,8]{3,4,2,1,0:T(8,128)} %param.6) | copy-start | bytes 110596
  7.2 48.9 %copy-start.6 = (f32[3,8,16,8]{2,3,1,0:T(8,128)S(1)}, f32[3,8,16,8]{2,3,1,0:T(8,128)}, u32[]{:S(2)}) copy-start(f32[3,8,16,8]{2,3,1,0:T(8,128)} %param.5) | copy-start | bytes 36868
  7.2 216.6 %all-gather.2.cloned.1.call-start = ((), (), s32[]{:S(2)}) async-start(), calls=%async_computation.1 | async-start | bytes 13369344 | tf_op jit(solution)/shard_map/all_gather | solution.py:86
  11.2 3.1 collective-permute-start
  14.4 6.2 %collective-permute-start.1 = (f32[128,128]{0,1:T(8,128)S(1)}, f32[128,128]{0,1:T(8,128)S(1)}, u32[]{:S(2)}, u32[]{:S(2)}) collective-permute-start(f32[128,128]{0,1:T(8,128)S(1)} %add.60), channel_id=1, source_target_pairs={{0,32},{16,48},{32,0},{48,16},{64,96},{80,112},{96,64},{112,80},{1... | collective-permute-start | bytes 196616 | tf_op jit(solution)/shard_map/ppermute | solution.py:11
  20.6 7.7 %collective-permute-start.2 = (f32[128,128]{0,1:T(8,128)S(1)}, f32[128,128]{0,1:T(8,128)S(1)}, u32[]{:S(2)}, u32[]{:S(2)}) collective-permute-start(f32[128,128]{0,1:T(8,128)S(1)} %add.61), channel_id=1, source_target_pairs={{0,64},{16,80},{32,96},{48,112},{64,0},{80,16},{96,32},{112,48},{1... | collective-permute-start | bytes 196616 | tf_op jit(solution)/shard_map/ppermute | solution.py:11
  28.4 14.0 %collective-permute-start.3 = (f32[128,128]{0,1:T(8,128)S(1)}, f32[128,128]{0,1:T(8,128)S(1)}, u32[]{:S(2)}, u32[]{:S(2)}) collective-permute-start(f32[128,128]{0,1:T(8,128)S(1)} %add.62), channel_id=1, source_target_pairs={{0,128},{16,144},{32,160},{48,176},{64,192},{80,208},{96,224},{112... | collective-permute-start | bytes 196616 | tf_op jit(solution)/shard_map/ppermute | solution.py:11
  42.4 17.4 %collective-permute-start.4 = (f32[128,128]{0,1:T(8,128)S(1)}, f32[128,128]{0,1:T(8,128)S(1)}, u32[]{:S(2)}, u32[]{:S(2)}) collective-permute-start(f32[128,128]{0,1:T(8,128)S(1)} %add.63), channel_id=1, source_target_pairs={{0,256},{16,272},{32,288},{48,304},{64,320},{80,336},{96,352},{112... | collective-permute-start | bytes 196616 | tf_op jit(solution)/shard_map/ppermute | solution.py:11
  89.0 7.0 %copy-start.1 = (f32[3,8,16,8,128]{4,2,3,1,0:T(8,128)}, f32[3,8,16,8,128]{4,2,3,1,0:T(8,128)S(1)}, u32[]{:S(2)}) copy-start(f32[3,8,16,8,128]{4,2,3,1,0:T(8,128)S(1)} %copy.30) | copy-start | bytes 4718596
  89.9 14.7 %collective-permute-start.5 = (f32[3,1,16,8,128]{4,2,3,1,0:T(8,128)}, f32[3,1,16,8,128]{4,2,3,1,0:T(8,128)}, u32[]{:S(2)}, u32[]{:S(2)}) collective-permute-start(f32[3,1,16,8,128]{4,2,3,1,0:T(8,128)} %get-tuple-element.11), channel_id=1, source_target_pairs={{16,0},{32,16},{48,32},{64,48},{80,64},{96,80},{112,96},{128,112},... | collective-permute-start | bytes 589832 | tf_op jit(solution)/shard_map/ppermute | solution.py:25
  91.2 13.4 %collective-permute-start.6 = (f32[3,1,16,8,128]{4,2,3,1,0:T(8,128)}, f32[3,1,16,8,128]{4,2,3,1,0:T(8,128)}, u32[]{:S(2)}, u32[]{:S(2)}) collective-permute-start(f32[3,1,16,8,128]{4,2,3,1,0:T(8,128)} %get-tuple-element.12), channel_id=1, source_target_pairs={{0,16},{16,32},{32,48},{48,64},{64,80},{80,96},{96,112},{112,128},... | collective-permute-start | bytes 589832 | tf_op jit(solution)/shard_map/ppermute | solution.py:23
  96.1 2.2 copy-start.4
  99.3 5.3 %copy-start.2 = (f32[3,8,16,8,128]{4,2,3,1,0:T(8,128)S(1)}, f32[3,8,16,8,128]{4,2,3,1,0:T(8,128)}, u32[]{:S(2)}) copy-start(f32[3,8,16,8,128]{4,2,3,1,0:T(8,128)} %copy-done.1) | copy-start | bytes 4718596
  109.5 237.8 %reduce-scatter.2.cloned.1.call-start = ((), (), s32[]{:S(2)}) async-start(), calls=%async_computation.2 | async-start | bytes 1081344 | tf_op jit(solution)/shard_map/reduce_scatter | solution.py:92
  223.8 16.2 %copy-start.3 = (f32[3,8,16,8,128]{4,2,3,1,0:T(8,128)S(1)}, f32[3,8,16,8,128]{4,2,3,1,0:T(8,128)}, u32[]{:S(2)}) copy-start(f32[3,8,16,8,128]{4,2,3,1,0:T(8,128)} %get-tuple-element.10) | copy-start | bytes 4718596
Sparse Core Ops, SparseCore 0:
  109.6 114.1 all-gather.1
  239.4 107.9 reduce-scatter.1
